TPU v7x, 32 devices: a whole 2x2x4 slice. The times are simulated.
32 devices in a mesh: section: 4 (over y, x), strip: 8 (over z, core).
Axes of the slice: x: 2, y: 2, z: 4, core: 2. Of those that a mesh axis runs over, the one named last changes fastest.
Arguments:
- images: bfloat16 [2, 32, 32, 256], P(None, 'strip'), may hold values from -6 to 6
- conv_first: bfloat16 [4, 9, 256, 256], P('section'), may hold values from -0.1875 to 0.1875
- conv_skip: bfloat16 [4, 9, 256, 256], P('section'), may hold values from -0.09375 to 0.09375
- conv_second: bfloat16 [4, 9, 256, 256], P('section'), may hold values from -0.1875 to 0.1875
- bias_first: float32 [4, 256], P('section'), may hold values from -0.8 to 0.8
- bias_second: float32 [4, 256], P('section'), may hold values from -0.8 to 0.8
Outputs:
- activations: bfloat16 [4, 2, 32, 32, 256], P('section', None, 'strip')
All inputs are finite; a program needn't handle non-finite values.
Results may differ from a plain program's by a relative error of at most 0.02.
Values may be sent and summed in bfloat16 or wider, within the bound.
A program may use at most 64 MiB of HBM per device.

v0:
```python
import functools

import jax
import jax.numpy as jnp
from jax import lax
from jax.experimental import pallas as pl
from jax.experimental.pallas import tpu as pltpu
from jax.sharding import PartitionSpec as P

MESH = pl.DeviceIdType.MESH
HALO = 2


def kernel(
    sections, strips,
    images, conv_first, conv_skip, conv_second, bias_first, bias_second,
    out,
    first_w, skip_w, second_w, first_b, second_b,
    land, skip_land, result, hidden_map, pre,
    weight_sem, image_sem, own_send, edge_send, edge_recv, skip_edge_send, skip_edge_recv, land_send, land_recv, skip_send, skip_recv, out_sem,
):
    section = lax.axis_index("section")
    strip = lax.axis_index("strip")
    micro, rows, cols, channels = result.shape
    middle = sections // 2
    is_first = section == 0
    has_next = section + 1 < sections
    has_above = strip > 0
    has_below = strip + 1 < strips
    sends_skip = (section > 0) & (section < middle)
    takes_skip = section > middle
    mirror = sections - section

    weights = (
        pltpu.make_async_copy(conv_first.at[0], first_w, weight_sem.at[0]),
        pltpu.make_async_copy(conv_second.at[0], second_w, weight_sem.at[1]),
        pltpu.make_async_copy(bias_first, first_b, weight_sem.at[2]),
        pltpu.make_async_copy(bias_second, second_b, weight_sem.at[3]),
    )
    skip_weight = pltpu.make_async_copy(conv_skip.at[0], skip_w, weight_sem.at[4])
    own_rows = pltpu.make_async_copy(images, land.at[:, pl.ds(HALO, rows)], image_sem)

    even = lax.rem(strip, 2) == 0
    inner = jnp.where(even, strip + 1, strip - 1)
    outer = jnp.where(even, strip - 1, strip + 1)
    has_inner = inner < strips
    has_outer = jnp.where(even, has_above, has_below)
    half = rows // 2
    inner_row = jnp.where(even, rows - half, 0)
    outer_row = jnp.where(even, 0, rows - half)
    inner_edge = jnp.where(even, rows - HALO, 0)
    outer_edge = jnp.where(even, 0, rows - HALO)
    inner_halo = jnp.where(even, 0, HALO + rows)
    outer_halo = jnp.where(even, HALO + rows, 0)

    def halves(m):
        return [pltpu.make_async_remote_copy(
            src_ref=result.at[m, pl.ds(row, half)], dst_ref=land.at[m, pl.ds(HALO + row, half)],
            send_sem=land_send.at[m, part], recv_sem=land_recv.at[m, part],
            device_id=(section + 1, strip), device_id_type=MESH)
            for part, row in enumerate((inner_row, outer_row))]

    def edge(m, source, to_section, part):
        send = edge_send if source is result else own_send
        row, halo, to_strip = ((inner_edge, inner_halo, inner), (outer_edge, outer_halo, outer))[part]
        return pltpu.make_async_remote_copy(
            src_ref=source.at[m, pl.ds(row, HALO)], dst_ref=land.at[m, pl.ds(halo, HALO)],
            send_sem=send.at[m, part], recv_sem=edge_recv.at[m, part],
            device_id=(to_section, to_strip), device_id_type=MESH)

    def start_outer(m, source, to_section):
        @pl.when(has_outer)
        def _():
            edge(m, source, to_section, 1).start()

    def start_inner(m, source):
        @pl.when(has_inner)
        def _():
            edge(m, source, section, 0).start()

    def sent_outer(m, source):
        @pl.when(has_outer)
        def _():
            edge(m, source, section, 1).wait_send()

    def sent_inner(m):
        @pl.when(has_inner)
        def _():
            edge(m, images, section, 0).wait_send()

    def skip_edge(m, part):
        row, halo, to_strip = ((inner_edge, inner_halo, inner), (outer_edge, outer_halo, outer))[part]
        return pltpu.make_async_remote_copy(
            src_ref=skip_land.at[m, pl.ds(HALO + row, HALO)], dst_ref=skip_land.at[m, pl.ds(halo, HALO)],
            send_sem=skip_edge_send.at[m, part], recv_sem=skip_edge_recv.at[m, part],
            device_id=(section, to_strip), device_id_type=MESH)

    beside = ((has_inner, 0), (has_outer, 1))

    landed = land.at[:, pl.ds(HALO, rows)]

    def skipped(m):
        return pltpu.make_async_remote_copy(
            src_ref=land.at[m, pl.ds(HALO, rows)], dst_ref=skip_land.at[m, pl.ds(HALO, rows)],
            send_sem=skip_send.at[m], recv_sem=skip_recv.at[m],
            device_id=(mirror, strip), device_id_type=MESH)

    for copy in weights:
        copy.start()
    pl.when(section >= middle)(skip_weight.start)
    pl.when(is_first)(own_rows.start)

    barrier = pltpu.get_barrier_semaphore()

    def greet(condition, to_section, to_strip):
        @pl.when(condition)
        def _():
            pl.semaphore_signal(barrier, inc=1, device_id=(to_section, to_strip), device_id_type=MESH)

    greet(has_inner, section, inner)
    greet(has_outer, jnp.where(is_first, section, section - 1), outer)
    greet(section > 0, section - 1, strip)
    greet(takes_skip, mirror, strip)
    greet(takes_skip & has_outer, section, outer)
    inner_count, outer_count = has_inner.astype(jnp.int32), has_outer.astype(jnp.int32)
    expected = (
        inner_count
        + jnp.where(is_first | takes_skip, outer_count, 0)
        + jnp.where(has_next, outer_count + 1, 0)
        + jnp.where(sends_skip, 1, 0)
    )

    @pl.when(expected > 0)
    def _():
        pl.semaphore_wait(barrier, expected)

    @pl.when(is_first)
    def _():
        for m in range(micro):
            start_outer(m, images, section)
            start_inner(m, images)

    blank = jnp.zeros((micro, HALO, cols, channels), land.dtype)

    @pl.when(jnp.logical_not(has_above))
    def _():
        land[:, 0:HALO] = blank
        skip_land[:, 0:HALO] = blank

    @pl.when(jnp.logical_not(has_below))
    def _():
        land[:, HALO + rows:] = blank
        skip_land[:, HALO + rows:] = blank

    pl.when(section >= middle)(skip_weight.wait)
    for copy in weights:
        copy.wait()

    @pl.when(section == middle)
    def _():
        def add(tap, carry):
            total = first_w[tap].astype(jnp.float32) + skip_w[tap].astype(jnp.float32)
            first_w[tap] = total.astype(first_w.dtype)
            return carry
        lax.fori_loop(0, 9, add, 0)

    def convolve(window, weight, out_rows):
        size = out_rows * cols
        shape = (out_rows, cols, channels)
        read = jnp.concatenate([window(a).reshape(size, channels) for a in range(3)], axis=1)
        column = lax.broadcasted_iota(jnp.int32, shape, 1)

        def product(b):
            taps = jnp.concatenate([weight[3 * a + b] for a in range(3)], axis=0)
            return jnp.dot(read, taps, preferred_element_type=jnp.float32)

        def moved(value, distance, edge_column):
            rolled = pltpu.roll(value, distance % size, axis=0).reshape(shape)
            return jnp.where(column == edge_column, 0.0, rolled)

        left = moved(product(0), 1, 0)
        right = moved(product(2), -1, cols - 1)
        return left + right + product(1).reshape(shape)

    hidden_rows = rows + 2
    first_bias = first_b[...].reshape(1, 1, channels)
    second_bias = second_b[...].reshape(1, 1, channels)

    @pl.when(takes_skip)
    def _():
        for m in range(micro):
            skipped(m).wait_recv()
            for condition, part in beside:
                pl.when(condition)(skip_edge(m, part).start)

        def skip_step(m, carry):
            for condition, part in beside:
                pl.when(condition)(skip_edge(m, part).wait_recv)
            pre[m] = first_bias + convolve(
                lambda a: skip_land[m, pl.ds(a, hidden_rows)], skip_w, hidden_rows)
            return carry

        lax.fori_loop(0, micro, skip_step, 0)

    @pl.when(jnp.logical_not(takes_skip))
    def _():
        pre[...] = jnp.broadcast_to(first_bias, pre.shape)

    pl.when(is_first)(own_rows.wait)

    def hide(m, begin, count):
        hidden = convolve(lambda a: land[m, pl.ds(begin + a, count)], first_w, count)
        hidden = jnp.maximum(hidden + pre[m, pl.ds(begin, count)], 0.0)
        row = begin + lax.broadcasted_iota(jnp.int32, hidden.shape, 0)
        least = jnp.where(has_above, 0, 1)
        most = jnp.where(has_below, hidden_rows, hidden_rows - 1)
        hidden = jnp.where((row >= least) & (row < most), hidden, 0.0)
        hidden_map[pl.ds(begin, count)] = hidden.astype(jnp.bfloat16)

    def finish(m, begin):
        final = convolve(lambda a: hidden_map[pl.ds(begin + a, half)], second_w, half)
        result[m, pl.ds(begin, half)] = jnp.maximum(final + second_bias, 0.0).astype(jnp.bfloat16)

    def step(m, carry):
        @pl.when(section > 0)
        def _():
            inner_half, outer_half = halves(m)
            inner_half.wait_recv()
            start_inner(m, landed)
            outer_half.wait_recv()

        @pl.when(sends_skip)
        def _():
            skipped(m).start()

        @pl.when(has_inner)
        def _():
            edge(m, result, section, 0).wait_recv()

        inner_half, outer_half = halves(m)
        hide(m, jnp.where(even, HALO, 0), rows)
        finish(m, inner_row)
        pl.when(has_next)(inner_half.start)

        @pl.when(has_outer)
        def _():
            edge(m, result, section, 1).wait_recv()

        hide(m, jnp.where(even, 0, rows), HALO)
        finish(m, outer_row)

        @pl.when(has_next)
        def _():
            start_outer(m, result, section + 1)
            outer_half.start()

        pltpu.make_async_copy(result.at[m], out.at[0, m], out_sem.at[m]).start()
        return carry

    lax.fori_loop(0, micro, step, 0)

    for m in range(micro):
        pltpu.make_async_copy(result.at[m], out.at[0, m], out_sem.at[m]).wait()

        sent_inner(m)

        @pl.when(takes_skip)
        def _():
            for condition, part in beside:
                pl.when(condition)(skip_edge(m, part).wait_send)

        @pl.when(is_first)
        def _():
            sent_outer(m, images)

        @pl.when(has_next)
        def _():
            for copy in halves(m):
                copy.wait_send()
            sent_outer(m, result)

        @pl.when(sends_skip)
        def _():
            skipped(m).wait_send()


def body(images, conv_first, conv_skip, conv_second, bias_first, bias_second):
    sections = lax.axis_size("section")
    strips = lax.axis_size("strip")
    arguments = (images, conv_first, conv_skip, conv_second, bias_first, bias_second)
    micro, rows, cols, channels = images.shape
    padded = (micro, rows + 2 * HALO, cols, channels)
    weight = conv_first.shape[1:]
    copies = pltpu.SemaphoreType.DMA((micro, 2))
    pixels = rows * cols
    flops = 2 * micro * 2 * pixels * channels * channels * 9
    return pl.pallas_call(
        functools.partial(kernel, sections, strips),
        out_shape=jax.ShapeDtypeStruct((1, micro, rows, cols, channels), jnp.bfloat16),
        in_specs=[pl.BlockSpec(memory_space=pltpu.HBM)] * 6,
        out_specs=pl.BlockSpec(memory_space=pltpu.HBM),
        scratch_shapes=[
            pltpu.VMEM(weight, jnp.bfloat16),
            pltpu.VMEM(weight, jnp.bfloat16),
            pltpu.VMEM(weight, jnp.bfloat16),
            pltpu.VMEM((1, channels), jnp.float32),
            pltpu.VMEM((1, channels), jnp.float32),
            pltpu.VMEM(padded, jnp.bfloat16),
            pltpu.VMEM(padded, jnp.bfloat16),
            pltpu.VMEM((micro, rows, cols, channels), jnp.bfloat16),
            pltpu.VMEM((rows + 2, cols, channels), jnp.bfloat16),
            pltpu.VMEM((micro, rows + 2, cols, channels), jnp.float32),
            pltpu.SemaphoreType.DMA((5,)),
            pltpu.SemaphoreType.DMA,
            copies, copies, copies, copies, copies, copies, copies,
            pltpu.SemaphoreType.DMA((micro,)),
            pltpu.SemaphoreType.DMA((micro,)),
            pltpu.SemaphoreType.DMA((micro,)),
        ],
        compiler_params=pltpu.CompilerParams(
            collective_id=0, has_side_effects=True, vmem_limit_bytes=32 * 1024 * 1024
        ),
        cost_estimate=pl.CostEstimate(
            flops=flops, bytes_accessed=3 * conv_first.size * 2, transcendentals=0
        ),
    )(*[pltpu.with_memory_space_constraint(value, pltpu.HBM) for value in arguments])


def solution(mesh):
    placed = (
        P(None, "strip", None, None),
        P("section", None, None, None),
        P("section", None, None, None),
        P("section", None, None, None),
        P("section", None),
        P("section", None),
    )
    return jax.shard_map(
        body,
        mesh=mesh,
        in_specs=placed,
        out_specs=P("section", None, "strip", None, None),
        check_vma=False,
    )
```

profile of v0, /device:TPU:23, one launch (start us, length us, event | category | flops | bytes accessed | tf_op | source)
XLA Modules:
  0.0 23.9 jit_solution(5038817950896589242)
XLA Ops:
  0.0 23.2 %shard_map.64 = bf16[1,2,4,32,256]{4,3,2,1,0:T(8,128)(2,1)S(1)} custom-call(bf16[2,4,32,256]{3,2,1,0:T(8,128)(2,1)} %images.1, bf16[1,9,256,256]{3,2,1,0:T(8,128)(2,1)} %conv_first.1, bf16[1,9,256,256]{3,2,1,0:T(8,128)(2,1)} %conv_skip.1, bf16[1,9,256,256]{3,2,1,0:T(8,128)(2,1)} %conv_second.1, f32[1,256]{1,0:T(1,128)} %bias_first.1, f32[1,256]{1,0:T(1,128)} %bias_second.1), custom_call_target="tpu_custom_call" | custom-call | flops 603979776 | bytes 3538944 | tf_op jit(solution)/shard_map/pallas_call | solution.py:297
  23.2 0.7 %copy.8 = bf16[1,2,4,32,256]{4,3,2,1,0:T(8,128)(2,1)} copy(bf16[1,2,4,32,256]{4,3,2,1,0:T(8,128)(2,1)S(1)} %shard_map.64) | data formatting | bytes 262144
where the time goes:
time: 24 us; the launch traced here: 23.9 us
  Pallas kernels  23.2 us (97%)
  local copies, waits for them, and re-layouts  0.66 us (3%)
    pallas_call x1, Pallas kernels, body(): pl.pallas_call(functools.partial(kernel, sections, strips), out_shape=jax...  23.2 us
    unnamed x1, local copies, waits for them, and re-layouts  0.66 us

commit v1 on v0

--- a/solution.py
+++ b/solution.py
@@ -53,6 +53,8 @@
     inner_halo = jnp.where(even, 0, HALO + rows)
     outer_halo = jnp.where(even, HALO + rows, 0)
 
+    landed = land.at[:, pl.ds(HALO, rows)]
+
     def halves(m):
         return [pltpu.make_async_remote_copy(
             src_ref=result.at[m, pl.ds(row, half)], dst_ref=land.at[m, pl.ds(HALO + row, half)],
@@ -73,10 +75,10 @@
         def _():
             edge(m, source, to_section, 1).start()
 
-    def start_inner(m, source):
+    def start_inner(m):
         @pl.when(has_inner)
         def _():
-            edge(m, source, section, 0).start()
+            edge(m, landed, section, 0).start()
 
     def sent_outer(m, source):
         @pl.when(has_outer)
@@ -86,7 +88,7 @@
     def sent_inner(m):
         @pl.when(has_inner)
         def _():
-            edge(m, images, section, 0).wait_send()
+            edge(m, landed, section, 0).wait_send()
 
     def skip_edge(m, part):
         row, halo, to_strip = ((inner_edge, inner_halo, inner), (outer_edge, outer_halo, outer))[part]
@@ -97,18 +99,16 @@
 
     beside = ((has_inner, 0), (has_outer, 1))
 
-    landed = land.at[:, pl.ds(HALO, rows)]
-
     def skipped(m):
         return pltpu.make_async_remote_copy(
             src_ref=land.at[m, pl.ds(HALO, rows)], dst_ref=skip_land.at[m, pl.ds(HALO, rows)],
             send_sem=skip_send.at[m], recv_sem=skip_recv.at[m],
             device_id=(mirror, strip), device_id_type=MESH)
 
+    pl.when(is_first)(own_rows.start)
     for copy in weights:
         copy.start()
     pl.when(section >= middle)(skip_weight.start)
-    pl.when(is_first)(own_rows.start)
 
     barrier = pltpu.get_barrier_semaphore()
 
@@ -136,9 +136,10 @@
 
     @pl.when(is_first)
     def _():
+        own_rows.wait()
         for m in range(micro):
-            start_outer(m, images, section)
-            start_inner(m, images)
+            start_outer(m, landed, section)
+            start_inner(m)
 
     blank = jnp.zeros((micro, HALO, cols, channels), land.dtype)
 
@@ -206,7 +207,6 @@
     def _():
         pre[...] = jnp.broadcast_to(first_bias, pre.shape)
 
-    pl.when(is_first)(own_rows.wait)
 
     def hide(m, begin, count):
         hidden = convolve(lambda a: land[m, pl.ds(begin + a, count)], first_w, count)
@@ -215,32 +215,37 @@
         least = jnp.where(has_above, 0, 1)
         most = jnp.where(has_below, hidden_rows, hidden_rows - 1)
         hidden = jnp.where((row >= least) & (row < most), hidden, 0.0)
-        hidden_map[pl.ds(begin, count)] = hidden.astype(jnp.bfloat16)
+        hidden_map[m, pl.ds(begin, count)] = hidden.astype(jnp.bfloat16)
 
     def finish(m, begin):
-        final = convolve(lambda a: hidden_map[pl.ds(begin + a, half)], second_w, half)
+        final = convolve(lambda a: hidden_map[m, pl.ds(begin + a, half)], second_w, half)
         result[m, pl.ds(begin, half)] = jnp.maximum(final + second_bias, 0.0).astype(jnp.bfloat16)
+
+    def inside(m, carry=0):
+        @pl.when(has_inner)
+        def _():
+            edge(m, landed, section, 0).wait_recv()
+
+        hide(m, jnp.where(even, HALO, 0), rows)
+        finish(m, inner_row)
+        pl.when(has_next)(halves(m)[0].start)
+        return carry
+
+    @pl.when(is_first)
+    def _():
+        lax.fori_loop(0, micro, inside, 0)
 
     def step(m, carry):
         @pl.when(section > 0)
         def _():
             inner_half, outer_half = halves(m)
             inner_half.wait_recv()
-            start_inner(m, landed)
+            start_inner(m)
             outer_half.wait_recv()
-
-        @pl.when(sends_skip)
-        def _():
-            skipped(m).start()
-
-        @pl.when(has_inner)
-        def _():
-            edge(m, result, section, 0).wait_recv()
-
-        inner_half, outer_half = halves(m)
-        hide(m, jnp.where(even, HALO, 0), rows)
-        finish(m, inner_row)
-        pl.when(has_next)(inner_half.start)
+            pl.when(sends_skip)(skipped(m).start)
+            inside(m)
+
+        outer_half = halves(m)[1]
 
         @pl.when(has_outer)
         def _():
@@ -251,8 +256,8 @@
 
         @pl.when(has_next)
         def _():
+            outer_half.start()
             start_outer(m, result, section + 1)
-            outer_half.start()
 
         pltpu.make_async_copy(result.at[m], out.at[0, m], out_sem.at[m]).start()
         return carry
@@ -271,7 +276,7 @@
 
         @pl.when(is_first)
         def _():
-            sent_outer(m, images)
+            sent_outer(m, landed)
 
         @pl.when(has_next)
         def _():
@@ -308,7 +313,7 @@
             pltpu.VMEM(padded, jnp.bfloat16),
             pltpu.VMEM(padded, jnp.bfloat16),
             pltpu.VMEM((micro, rows, cols, channels), jnp.bfloat16),
-            pltpu.VMEM((rows + 2, cols, channels), jnp.bfloat16),
+            pltpu.VMEM((micro, rows + 2, cols, channels), jnp.bfloat16),
             pltpu.VMEM((micro, rows + 2, cols, channels), jnp.float32),
             pltpu.SemaphoreType.DMA((5,)),
             pltpu.SemaphoreType.DMA,

time: 24 us -> 25 us (1.042)
  Pallas kernels: 23.2 us -> 24.2 us
    pallas_call x1, Pallas kernels: 23.2 us -> 24.2 us  [body(): pl.pallas_call(functools.partial(kernel, sections, strips), out_shape=jax...]
where the time goes in v1:
time: 25 us; the launch traced here: 24.9 us
  Pallas kernels  24.2 us (97%)
  local copies, waits for them, and re-layouts  0.66 us (3%)
    pallas_call x1, Pallas kernels, body(): pl.pallas_call(functools.partial(kernel, sections, strips), out_shape=jax...  24.2 us
    unnamed x1, local copies, waits for them, and re-layouts  0.66 us

profile of v1, /device:TPU:23, one launch (start us, length us, event | category | flops | bytes accessed | tf_op | source)
XLA Modules:
  0.0 24.9 jit_solution(9674811280979205869)
XLA Ops:
  0.0 24.2 %shard_map.64 = bf16[1,2,4,32,256]{4,3,2,1,0:T(8,128)(2,1)S(1)} custom-call(bf16[2,4,32,256]{3,2,1,0:T(8,128)(2,1)} %images.1, bf16[1,9,256,256]{3,2,1,0:T(8,128)(2,1)} %conv_first.1, bf16[1,9,256,256]{3,2,1,0:T(8,128)(2,1)} %conv_skip.1, bf16[1,9,256,256]{3,2,1,0:T(8,128)(2,1)} %conv_second.1, f32[1,256]{1,0:T(1,128)} %bias_first.1, f32[1,256]{1,0:T(1,128)} %bias_second.1), custom_call_target="tpu_custom_call" | custom-call | flops 603979776 | bytes 3538944 | tf_op jit(solution)/shard_map/pallas_call | solution.py:302
  24.2 0.7 %copy.8 = bf16[1,2,4,32,256]{4,3,2,1,0:T(8,128)(2,1)} copy(bf16[1,2,4,32,256]{4,3,2,1,0:T(8,128)(2,1)S(1)} %shard_map.64) | data formatting | bytes 262144

commit v2 on v0

--- a/solution.py
+++ b/solution.py
@@ -53,6 +53,8 @@
     inner_halo = jnp.where(even, 0, HALO + rows)
     outer_halo = jnp.where(even, HALO + rows, 0)
 
+    landed = land.at[:, pl.ds(HALO, rows)]
+
     def halves(m):
         return [pltpu.make_async_remote_copy(
             src_ref=result.at[m, pl.ds(row, half)], dst_ref=land.at[m, pl.ds(HALO + row, half)],
@@ -73,10 +75,10 @@
         def _():
             edge(m, source, to_section, 1).start()
 
-    def start_inner(m, source):
+    def start_inner(m):
         @pl.when(has_inner)
         def _():
-            edge(m, source, section, 0).start()
+            edge(m, landed, section, 0).start()
 
     def sent_outer(m, source):
         @pl.when(has_outer)
@@ -86,7 +88,7 @@
     def sent_inner(m):
         @pl.when(has_inner)
         def _():
-            edge(m, images, section, 0).wait_send()
+            edge(m, landed, section, 0).wait_send()
 
     def skip_edge(m, part):
         row, halo, to_strip = ((inner_edge, inner_halo, inner), (outer_edge, outer_halo, outer))[part]
@@ -97,7 +99,10 @@
 
     beside = ((has_inner, 0), (has_outer, 1))
 
-    landed = land.at[:, pl.ds(HALO, rows)]
+    def written(m):
+        return [pltpu.make_async_copy(
+            result.at[m, pl.ds(row, half)], out.at[0, m, pl.ds(row, half)], out_sem.at[m, part])
+            for part, row in enumerate((inner_row, outer_row))]
 
     def skipped(m):
         return pltpu.make_async_remote_copy(
@@ -105,10 +110,10 @@
             send_sem=skip_send.at[m], recv_sem=skip_recv.at[m],
             device_id=(mirror, strip), device_id_type=MESH)
 
+    pl.when(is_first)(own_rows.start)
     for copy in weights:
         copy.start()
     pl.when(section >= middle)(skip_weight.start)
-    pl.when(is_first)(own_rows.start)
 
     barrier = pltpu.get_barrier_semaphore()
 
@@ -136,9 +141,11 @@
 
     @pl.when(is_first)
     def _():
+        own_rows.wait()
         for m in range(micro):
-            start_outer(m, images, section)
-            start_inner(m, images)
+            start_outer(m, landed, section)
+        for m in range(micro):
+            start_inner(m)
 
     blank = jnp.zeros((micro, HALO, cols, channels), land.dtype)
 
@@ -206,7 +213,6 @@
     def _():
         pre[...] = jnp.broadcast_to(first_bias, pre.shape)
 
-    pl.when(is_first)(own_rows.wait)
 
     def hide(m, begin, count):
         hidden = convolve(lambda a: land[m, pl.ds(begin + a, count)], first_w, count)
@@ -226,7 +232,7 @@
         def _():
             inner_half, outer_half = halves(m)
             inner_half.wait_recv()
-            start_inner(m, landed)
+            start_inner(m)
             outer_half.wait_recv()
 
         @pl.when(sends_skip)
@@ -241,6 +247,7 @@
         hide(m, jnp.where(even, HALO, 0), rows)
         finish(m, inner_row)
         pl.when(has_next)(inner_half.start)
+        written(m)[0].start()
 
         @pl.when(has_outer)
         def _():
@@ -254,13 +261,14 @@
             start_outer(m, result, section + 1)
             outer_half.start()
 
-        pltpu.make_async_copy(result.at[m], out.at[0, m], out_sem.at[m]).start()
+        written(m)[1].start()
         return carry
 
     lax.fori_loop(0, micro, step, 0)
 
     for m in range(micro):
-        pltpu.make_async_copy(result.at[m], out.at[0, m], out_sem.at[m]).wait()
+        for copy in written(m):
+            copy.wait()
 
         sent_inner(m)
 
@@ -271,7 +279,7 @@
 
         @pl.when(is_first)
         def _():
-            sent_outer(m, images)
+            sent_outer(m, landed)
 
         @pl.when(has_next)
         def _():
@@ -315,7 +323,7 @@
             copies, copies, copies, copies, copies, copies, copies,
             pltpu.SemaphoreType.DMA((micro,)),
             pltpu.SemaphoreType.DMA((micro,)),
-            pltpu.SemaphoreType.DMA((micro,)),
+            copies,
         ],
         compiler_params=pltpu.CompilerParams(
             collective_id=0, has_side_effects=True, vmem_limit_bytes=32 * 1024 * 1024

time: 24 us -> 23.8 us (level)
  no operation moved by 1% of the time
where the time goes in v2:
time: 23.8 us; the launch traced here: 23.7 us
  Pallas kernels  23 us (97%)
  local copies, waits for them, and re-layouts  0.66 us (3%)
    pallas_call x1, Pallas kernels, body(): pl.pallas_call(functools.partial(kernel, sections, strips), out_shape=jax...  23 us
    unnamed x1, local copies, waits for them, and re-layouts  0.66 us

profile of v2, /device:TPU:23, one launch (start us, length us, event | category | flops | bytes accessed | tf_op | source)
XLA Modules:
  0.0 23.7 jit_solution(5099627408246442708)
XLA Ops:
  0.0 23.0 %shard_map.64 = bf16[1,2,4,32,256]{4,3,2,1,0:T(8,128)(2,1)S(1)} custom-call(bf16[2,4,32,256]{3,2,1,0:T(8,128)(2,1)} %images.1, bf16[1,9,256,256]{3,2,1,0:T(8,128)(2,1)} %conv_first.1, bf16[1,9,256,256]{3,2,1,0:T(8,128)(2,1)} %conv_skip.1, bf16[1,9,256,256]{3,2,1,0:T(8,128)(2,1)} %conv_second.1, f32[1,256]{1,0:T(1,128)} %bias_first.1, f32[1,256]{1,0:T(1,128)} %bias_second.1), custom_call_target="tpu_custom_call" | custom-call | flops 603979776 | bytes 3538944 | tf_op jit(solution)/shard_map/pallas_call | solution.py:305
  23.0 0.7 %copy.8 = bf16[1,2,4,32,256]{4,3,2,1,0:T(8,128)(2,1)} copy(bf16[1,2,4,32,256]{4,3,2,1,0:T(8,128)(2,1)S(1)} %shard_map.64) | data formatting | bytes 262144

commit v3 on v2

--- a/solution.py
+++ b/solution.py
@@ -31,13 +31,18 @@
     takes_skip = section > middle
     mirror = sections - section
 
-    weights = (
-        pltpu.make_async_copy(conv_first.at[0], first_w, weight_sem.at[0]),
-        pltpu.make_async_copy(conv_second.at[0], second_w, weight_sem.at[1]),
-        pltpu.make_async_copy(bias_first, first_b, weight_sem.at[2]),
-        pltpu.make_async_copy(bias_second, second_b, weight_sem.at[3]),
-    )
-    skip_weight = pltpu.make_async_copy(conv_skip.at[0], skip_w, weight_sem.at[4])
+    def fetched(source, target, slot):
+        return [pltpu.make_async_copy(
+            source.at[0, pl.ds(3 * a, 3)], target.at[pl.ds(3 * a, 3)], weight_sem.at[slot, a])
+            for a in range(3)]
+
+    first_weights = fetched(conv_first, first_w, 0)
+    second_weights = fetched(conv_second, second_w, 1)
+    skip_weights = fetched(conv_skip, skip_w, 2)
+    biases = [
+        pltpu.make_async_copy(bias_first, first_b, weight_sem.at[3, 0]),
+        pltpu.make_async_copy(bias_second, second_b, weight_sem.at[3, 1]),
+    ]
     own_rows = pltpu.make_async_copy(images, land.at[:, pl.ds(HALO, rows)], image_sem)
 
     even = lax.rem(strip, 2) == 0
@@ -111,9 +116,13 @@
             device_id=(mirror, strip), device_id_type=MESH)
 
     pl.when(is_first)(own_rows.start)
-    for copy in weights:
+    for copy in first_weights + biases + second_weights:
         copy.start()
-    pl.when(section >= middle)(skip_weight.start)
+
+    @pl.when(section >= middle)
+    def _():
+        for copy in skip_weights:
+            copy.start()
 
     barrier = pltpu.get_barrier_semaphore()
 
@@ -159,9 +168,13 @@
         land[:, HALO + rows:] = blank
         skip_land[:, HALO + rows:] = blank
 
-    pl.when(section >= middle)(skip_weight.wait)
-    for copy in weights:
+    for copy in first_weights + biases:
         copy.wait()
+
+    @pl.when(section >= middle)
+    def _():
+        for copy in skip_weights:
+            copy.wait()
 
     @pl.when(section == middle)
     def _():
@@ -245,6 +258,12 @@
 
         inner_half, outer_half = halves(m)
         hide(m, jnp.where(even, HALO, 0), rows)
+
+        @pl.when(m == 0)
+        def _():
+            for copy in second_weights:
+                copy.wait()
+
         finish(m, inner_row)
         pl.when(has_next)(inner_half.start)
         written(m)[0].start()
@@ -318,7 +337,7 @@
             pltpu.VMEM((micro, rows, cols, channels), jnp.bfloat16),
             pltpu.VMEM((rows + 2, cols, channels), jnp.bfloat16),
             pltpu.VMEM((micro, rows + 2, cols, channels), jnp.float32),
-            pltpu.SemaphoreType.DMA((5,)),
+            pltpu.SemaphoreType.DMA((4, 3)),
             pltpu.SemaphoreType.DMA,
             copies, copies, copies, copies, copies, copies, copies,
             pltpu.SemaphoreType.DMA((micro,)),

time: 23.8 us -> 24.1 us (1.013)
  Pallas kernels: 23 us -> 23.3 us
    pallas_call x1, Pallas kernels: 23 us -> 23.3 us  [body(): pl.pallas_call(functools.partial(kernel, sections, strips), out_shape=jax...]
where the time goes in v3:
time: 24.1 us; the launch traced here: 24 us
  Pallas kernels  23.3 us (97%)
  local copies, waits for them, and re-layouts  0.66 us (3%)
    pallas_call x1, Pallas kernels, body(): pl.pallas_call(functools.partial(kernel, sections, strips), out_shape=jax...  23.3 us
    unnamed x1, local copies, waits for them, and re-layouts  0.66 us

profile of v3, /device:TPU:23, one launch (start us, length us, event | category | flops | bytes accessed | tf_op | source)
XLA Modules:
  0.0 24.0 jit_solution(3361490473823238587)
XLA Ops:
  0.0 23.3 %shard_map.64 = bf16[1,2,4,32,256]{4,3,2,1,0:T(8,128)(2,1)S(1)} custom-call(bf16[2,4,32,256]{3,2,1,0:T(8,128)(2,1)} %images.1, bf16[1,9,256,256]{3,2,1,0:T(8,128)(2,1)} %conv_first.1, bf16[1,9,256,256]{3,2,1,0:T(8,128)(2,1)} %conv_skip.1, bf16[1,9,256,256]{3,2,1,0:T(8,128)(2,1)} %conv_second.1, f32[1,256]{1,0:T(1,128)} %bias_first.1, f32[1,256]{1,0:T(1,128)} %bias_second.1), custom_call_target="tpu_custom_call" | custom-call | flops 603979776 | bytes 3538944 | tf_op jit(solution)/shard_map/pallas_call | solution.py:324
  23.3 0.7 %copy.8 = bf16[1,2,4,32,256]{4,3,2,1,0:T(8,128)(2,1)} copy(bf16[1,2,4,32,256]{4,3,2,1,0:T(8,128)(2,1)S(1)} %shard_map.64) | data formatting | bytes 262144

commit v4 on v2

--- a/solution.py
+++ b/solution.py
@@ -16,12 +16,13 @@
     images, conv_first, conv_skip, conv_second, bias_first, bias_second,
     out,
     first_w, skip_w, second_w, first_b, second_b,
-    land, skip_land, result, hidden_map, pre,
-    weight_sem, image_sem, own_send, edge_send, edge_recv, skip_edge_send, skip_edge_recv, land_send, land_recv, skip_send, skip_recv, out_sem,
+    land, skip_land, hidden_map, pre,
+    weight_sem, image_sem, own_send, edge_send, edge_recv, skip_edge_send, skip_edge_recv, land_send, land_recv, skip_send, skip_recv,
 ):
     section = lax.axis_index("section")
     strip = lax.axis_index("strip")
-    micro, rows, cols, channels = result.shape
+    result = out.at[0]
+    micro, rows, cols, channels = images.shape
     middle = sections // 2
     is_first = section == 0
     has_next = section + 1 < sections
@@ -99,11 +100,6 @@
 
     beside = ((has_inner, 0), (has_outer, 1))
 
-    def written(m):
-        return [pltpu.make_async_copy(
-            result.at[m, pl.ds(row, half)], out.at[0, m, pl.ds(row, half)], out_sem.at[m, part])
-            for part, row in enumerate((inner_row, outer_row))]
-
     def skipped(m):
         return pltpu.make_async_remote_copy(
             src_ref=land.at[m, pl.ds(HALO, rows)], dst_ref=skip_land.at[m, pl.ds(HALO, rows)],
@@ -247,7 +243,6 @@
         hide(m, jnp.where(even, HALO, 0), rows)
         finish(m, inner_row)
         pl.when(has_next)(inner_half.start)
-        written(m)[0].start()
 
         @pl.when(has_outer)
         def _():
@@ -261,15 +256,11 @@
             start_outer(m, result, section + 1)
             outer_half.start()
 
-        written(m)[1].start()
         return carry
 
     lax.fori_loop(0, micro, step, 0)
 
     for m in range(micro):
-        for copy in written(m):
-            copy.wait()
-
         sent_inner(m)
 
         @pl.when(takes_skip)
@@ -306,7 +297,7 @@
         functools.partial(kernel, sections, strips),
         out_shape=jax.ShapeDtypeStruct((1, micro, rows, cols, channels), jnp.bfloat16),
         in_specs=[pl.BlockSpec(memory_space=pltpu.HBM)] * 6,
-        out_specs=pl.BlockSpec(memory_space=pltpu.HBM),
+        out_specs=pl.BlockSpec(memory_space=pltpu.VMEM),
         scratch_shapes=[
             pltpu.VMEM(weight, jnp.bfloat16),
             pltpu.VMEM(weight, jnp.bfloat16),
@@ -315,7 +306,6 @@
             pltpu.VMEM((1, channels), jnp.float32),
             pltpu.VMEM(padded, jnp.bfloat16),
             pltpu.VMEM(padded, jnp.bfloat16),
-            pltpu.VMEM((micro, rows, cols, channels), jnp.bfloat16),
             pltpu.VMEM((rows + 2, cols, channels), jnp.bfloat16),
             pltpu.VMEM((micro, rows + 2, cols, channels), jnp.float32),
             pltpu.SemaphoreType.DMA((5,)),
@@ -323,7 +313,6 @@
             copies, copies, copies, copies, copies, copies, copies,
             pltpu.SemaphoreType.DMA((micro,)),
             pltpu.SemaphoreType.DMA((micro,)),
-            copies,
         ],
         compiler_params=pltpu.CompilerParams(
             collective_id=0, has_side_effects=True, vmem_limit_bytes=32 * 1024 * 1024

time: 23.8 us -> 23.8 us (level)
  no operation moved by 1% of the time
where the time goes in v4:
time: 23.8 us; the launch traced here: 23.6 us
  Pallas kernels  23 us (97%)
  local copies, waits for them, and re-layouts  0.66 us (3%)
    pallas_call x1, Pallas kernels, body(): pl.pallas_call(functools.partial(kernel, sections, strips), out_shape=jax...  23 us
    unnamed x1, local copies, waits for them, and re-layouts  0.66 us

profile of v4, /device:TPU:23, one launch (start us, length us, event | category | flops | bytes accessed | tf_op | source)
XLA Modules:
  0.0 23.6 jit_solution(290746104725057278)
XLA Ops:
  0.0 23.0 %shard_map.64 = bf16[1,2,4,32,256]{4,3,2,1,0:T(8,128)(2,1)S(1)} custom-call(bf16[2,4,32,256]{3,2,1,0:T(8,128)(2,1)} %images.1, bf16[1,9,256,256]{3,2,1,0:T(8,128)(2,1)} %conv_first.1, bf16[1,9,256,256]{3,2,1,0:T(8,128)(2,1)} %conv_skip.1, bf16[1,9,256,256]{3,2,1,0:T(8,128)(2,1)} %conv_second.1, f32[1,256]{1,0:T(1,128)} %bias_first.1, f32[1,256]{1,0:T(1,128)} %bias_second.1), custom_call_target="tpu_custom_call" | custom-call | flops 603979776 | bytes 3538944 | tf_op jit(solution)/shard_map/pallas_call | solution.py:296
  23.0 0.7 %copy.8 = bf16[1,2,4,32,256]{4,3,2,1,0:T(8,128)(2,1)} copy(bf16[1,2,4,32,256]{4,3,2,1,0:T(8,128)(2,1)S(1)} %shard_map.64) | data formatting | bytes 262144

commit v5 on v4

--- a/solution.py
+++ b/solution.py
@@ -231,10 +231,6 @@
             start_inner(m)
             outer_half.wait_recv()
 
-        @pl.when(sends_skip)
-        def _():
-            skipped(m).start()
-
         @pl.when(has_inner)
         def _():
             edge(m, result, section, 0).wait_recv()
@@ -243,6 +239,7 @@
         hide(m, jnp.where(even, HALO, 0), rows)
         finish(m, inner_row)
         pl.when(has_next)(inner_half.start)
+        pl.when(sends_skip)(skipped(m).start)
 
         @pl.when(has_outer)
         def _():

time: 23.8 us -> 24 us (level)
  no operation moved by 1% of the time
where the time goes in v5:
time: 24 us; the launch traced here: 23.6 us
  Pallas kernels  23 us (96%)
  local copies, waits for them, and re-layouts  0.66 us (3%)
    pallas_call x1, Pallas kernels, body(): pl.pallas_call(functools.partial(kernel, sections, strips), out_shape=jax...  23 us
    unnamed x1, local copies, waits for them, and re-layouts  0.66 us

profile of v5, /device:TPU:23, one launch (start us, length us, event | category | flops | bytes accessed | tf_op | source)
XLA Modules:
  0.0 23.6 jit_solution(10057088197924598045)
XLA Ops:
  0.0 23.0 %shard_map.64 = bf16[1,2,4,32,256]{4,3,2,1,0:T(8,128)(2,1)S(1)} custom-call(bf16[2,4,32,256]{3,2,1,0:T(8,128)(2,1)} %images.1, bf16[1,9,256,256]{3,2,1,0:T(8,128)(2,1)} %conv_first.1, bf16[1,9,256,256]{3,2,1,0:T(8,128)(2,1)} %conv_skip.1, bf16[1,9,256,256]{3,2,1,0:T(8,128)(2,1)} %conv_second.1, f32[1,256]{1,0:T(1,128)} %bias_first.1, f32[1,256]{1,0:T(1,128)} %bias_second.1), custom_call_target="tpu_custom_call" | custom-call | flops 603979776 | bytes 3538944 | tf_op jit(solution)/shard_map/pallas_call | solution.py:293
  23.0 0.7 %copy.8 = bf16[1,2,4,32,256]{4,3,2,1,0:T(8,128)(2,1)} copy(bf16[1,2,4,32,256]{4,3,2,1,0:T(8,128)(2,1)S(1)} %shard_map.64) | data formatting | bytes 262144
